TPU v7x, 512 devices: a whole 4x4x16 slice. The times are simulated.
512 devices in a mesh: seq: 64 (over y, z), head: 8 (over x, core).
Axes of the slice: x: 4, y: 4, z: 16, core: 2. Of those that a mesh axis runs over, the one named last changes fastest.
Arguments:
- queries: bfloat16 [32768, 16, 128], P('seq', 'head'), may hold values from -5 to 5
- keys: bfloat16 [32768, 16, 128], P('seq', 'head'), may hold values from -5 to 5
- values: bfloat16 [32768, 16, 128], P('seq', 'head'), may hold values from -6 to 6
- layer_grad: bfloat16 [32768, 2048], P('seq', 'head'), may hold values from -6 to 6
- out_proj: bfloat16 [16, 128, 2048], P('head'), may hold values from -0.125 to 0.125
- cluster: int32 [16, 32768], P('head', 'seq'), may hold values from 0 to 511, as said below
- slot: int32 [16, 32768], P('head', 'seq'), may hold values from 0 to 2, as said below
- tile_of: int32 [16, 512], P('head'), may hold values from 0 to 511, as said below
Outputs:
- query_grad: bfloat16 [32768, 16, 128], P('seq', 'head')
- key_grad: bfloat16 [32768, 16, 128], P('seq', 'head')
- value_grad: bfloat16 [32768, 16, 128], P('seq', 'head')
- centroid_sums: float32 [16, 512, 128], P('head', 'seq')
Inputs may be any that keep to these rules, and one draw needn't show every extreme that they name: For each head, among the 512 tokens of one device at most 3 are in one cluster, and at most 16 are in clusters whose tile_of values give the same owner (tile // 8); in every head one cluster has exactly 3 tokens on every device, and one owner exactly 16 from every device. `slot`: for each head and each device, the tokens of one cluster carry slots 0, 1, 2, ... in the order of their positions. `tile_of`: for each head a permutation of the clusters.
All inputs are finite; a program needn't handle non-finite values.
Results may differ from a plain program's by a relative error of at most 0.0087.
Values may be sent and summed in bfloat16 or wider, within the bound.
A program may use at most 64 MiB of HBM per device.

v0:
```python
import jax
import jax.numpy as jnp
from jax import lax
from jax.sharding import PartitionSpec as P


def tile_grads(query_tile, key_tile, value_tile, grad_tile, used_rows):
    factor = query_tile.shape[-1] ** (-0.5)
    scores = (
        jnp.einsum("brd,bcd->brc", query_tile, key_tile, preferred_element_type=jnp.float32)
        * factor
    )
    tile_rows = query_tile.shape[1]
    row_index = jnp.arange(tile_rows)[:, None]
    col_index = jnp.arange(tile_rows)[None, :]
    allowed = (
        (col_index <= row_index)[None] & (used_rows[:, :, None] > 0) & (used_rows[:, None, :] > 0)
    )
    row_max = jnp.max(jnp.where(allowed, scores, -1e30), axis=2, keepdims=True)
    weights = jnp.where(allowed, jnp.exp(scores - row_max), 0.0)
    row_total = jnp.where(used_rows > 0, jnp.sum(weights, axis=2), 1.0)
    weights = weights / row_total[:, :, None]
    weights_low = weights.astype(jnp.bfloat16)
    attended = jnp.einsum(
        "brc,bcd->brd", weights_low, value_tile, preferred_element_type=jnp.float32
    )
    diag_term = jnp.sum(grad_tile.astype(jnp.float32) * attended, axis=2)
    dprobs = jnp.einsum("brd,bcd->brc", grad_tile, value_tile, preferred_element_type=jnp.float32)
    dscores = (weights * (dprobs - diag_term[:, :, None])).astype(jnp.bfloat16)
    query_grad = (
        jnp.einsum("brc,bcd->brd", dscores, key_tile, preferred_element_type=jnp.float32) * factor
    ).astype(jnp.bfloat16)
    key_grad = (
        jnp.einsum("brc,brd->bcd", dscores, query_tile, preferred_element_type=jnp.float32) * factor
    ).astype(jnp.bfloat16)
    value_grad = jnp.einsum(
        "brc,brd->bcd", weights_low, grad_tile, preferred_element_type=jnp.float32
    ).astype(jnp.bfloat16)
    query_wide = query_tile.astype(jnp.float32)
    key_wide = key_tile.astype(jnp.float32)
    unit_query = query_wide * lax.rsqrt(
        jnp.sum(query_wide * query_wide, axis=2, keepdims=True) + 1e-06
    )
    unit_key = key_wide * lax.rsqrt(jnp.sum(key_wide * key_wide, axis=2, keepdims=True) + 1e-06)
    centroid = jnp.einsum("br,brd->bd", used_rows, unit_query + unit_key)
    return (query_grad, key_grad, value_grad, centroid)


def on_device(queries, keys, values, layer_grad, out_proj, cluster, slot, tile_of):
    token_count, head_count, head_size = queries.shape
    seq_count = lax.axis_size("seq")
    cluster_count = tile_of.shape[1]
    local_count = cluster_count // seq_count
    per_source = 3 * token_count // cluster_count
    capacity = seq_count * per_source
    block = out_proj
    out_grad = jnp.einsum(
        "tm,hdm->thd",
        lax.all_gather(layer_grad, "head", axis=1, tiled=True),
        block,
        preferred_element_type=jnp.float32,
    ).astype(jnp.bfloat16)
    cluster_ids = jnp.arange(cluster_count, dtype=jnp.int32)
    tile_index = jnp.sum(
        jnp.where(cluster[:, :, None] == cluster_ids, tile_of[:, None, :], 0), axis=2
    )
    target = tile_index // local_count
    local_tile = tile_index % local_count
    payload = jnp.transpose(jnp.stack([queries, keys, values, out_grad], axis=2), (1, 0, 2, 3))
    head_rows = jnp.arange(head_count)[:, None]
    buffer_row = local_tile * capacity + target * per_source + slot
    outbox = (
        jnp.zeros((head_count, local_count * capacity, 4, head_size), jnp.bfloat16)
        .at[head_rows, buffer_row]
        .set(payload)
    )
    used_flag = (
        jnp.zeros((head_count, local_count * capacity), jnp.int32).at[head_rows, buffer_row].set(1)
    )
    outgoing = (
        outbox.reshape(head_count, local_count, seq_count, per_source, 4, head_size),
        used_flag.reshape(head_count, local_count, seq_count, per_source),
    )
    received = (
        lax.all_to_all(outgoing[0], "seq", split_axis=2, concat_axis=2, tiled=True),
        lax.all_to_all(outgoing[1], "seq", split_axis=2, concat_axis=2, tiled=True),
    )
    items = received[0].shape[0]
    tiled = received[0].reshape(items, local_count, capacity, 4, head_size)
    used = received[1].reshape(items, local_count, capacity).astype(jnp.float32)
    gradients = []
    centroids = []
    for member in range(items):
        block = tiled[member]
        query_grad, key_grad, value_grad, centroid = tile_grads(
            block[:, :, 0], block[:, :, 1], block[:, :, 2], block[:, :, 3], used[member]
        )
        gradients.append(jnp.stack([query_grad, key_grad, value_grad], axis=2))
        centroids.append(centroid)
    gradients = jnp.stack(gradients)
    centroids = jnp.stack(centroids)
    outbound = gradients.reshape(items, local_count, seq_count, per_source, 3, head_size)
    outbound, centroids = (outbound, centroids)
    returned = lax.all_to_all(outbound, "seq", split_axis=2, concat_axis=2, tiled=True)
    back_rows = returned.reshape(head_count, local_count * capacity, 3, head_size)[
        head_rows, buffer_row
    ]
    back_rows = jnp.transpose(back_rows, (1, 0, 2, 3))
    return (back_rows[:, :, 0], back_rows[:, :, 1], back_rows[:, :, 2], centroids)


def solution(mesh):
    in_specs = (
        P("seq", "head", None),
        P("seq", "head", None),
        P("seq", "head", None),
        P("seq", "head"),
        P("head", None, None),
        P("head", "seq"),
        P("head", "seq"),
        P("head", None),
    )
    out_specs = (
        P("seq", "head", None),
        P("seq", "head", None),
        P("seq", "head", None),
        P("head", "seq", None),
    )
    return jax.shard_map(
        on_device, mesh=mesh, in_specs=in_specs, out_specs=out_specs, check_vma=False
    )
```

profile of v0, /device:TPU:6, one launch (start us, length us, event | category | flops | bytes accessed | tf_op | source)
XLA Modules:
  0.0 467.9 jit_solution(17614951180427451435)
XLA Ops:
  7.3 0.7 all-gather.2.cloned.1.call-update
  7.9 1.2 select_reduce_fusion
  9.1 0.7 or_bitcast_fusion
  9.8 0.7 multiply_reduce_fusion
  10.6 0.7 and_reduce_fusion
  11.4 4.3 scatter_custom_fusion
  15.7 0.3 reshape.129
  16.0 1.5 copy.98
  17.6 18.7 %all-to-all-start = ((s32[2,8,64,3]{1,0,3,2:T(2,128)}), s32[2,8,64,3]{1,0,3,2:T(2,128)S(1)}, u32[]{:S(2)}, u32[]{:S(2)}) async-start(s32[2,8,64,3]{1,0,3,2:T(2,128)} %copy.98), calls=%async_computation | async-start | bytes 393216 | tf_op jit(solution)/shard_map/all_to_all | solution.py:86
  36.5 12.4 %all-gather.2.cloned.1.call-done = bf16[512,2048]{1,0:T(8,128)(2,1)} async-done(((bf16[512,256]{1,0:T(8,128)(2,1)}), bf16[512,2048]{1,0:T(8,128)(2,1)}) %all-gather.2.cloned.1.call-update) | async-done | bytes 2097168 | tf_op jit(solution)/shard_map/all_gather | solution.py:59
  48.9 2.3 fusion.19
  51.2 0.1 pad_maximum_fusion
  51.4 0.8 copy.103
  52.2 2.5 broadcast.121
  54.7 95.1 %scatter_fusion = bf16[3072,4,128]{2,1,0:T(4,128)(2,1)} fusion(bf16[3072,4,128]{2,1,0:T(4,128)(2,1)} %broadcast.121, s32[1024]{0:T(1024)S(1)} %bitcast.142, bf16[1024,4,128]{2,1,0:T(4,128)(2,1)S(1)} %copy.103), kind=kCustom, calls=%fused_computation.2 | custom fusion | bytes 3149824
  149.8 5.3 %copy.104 = bf16[2,8,64,3,4,128]{5,4,3,1,0,2:T(4,128)(2,1)} copy(bf16[2,8,64,3,4,128]{5,4,3,2,1,0:T(4,128)(2,1)} %bitcast.124) | data formatting | bytes 6291456 | tf_op jit(solution)/shard_map/reshape | solution.py:81
  155.1 16.1 %all-to-all-start.1 = ((bf16[2,8,64,3,4,128]{5,4,3,1,0,2:T(4,128)(2,1)}), bf16[2,8,64,3,4,128]{5,4,3,1,0,2:T(4,128)(2,1)}, u32[]{:S(2)}, u32[]{:S(2)}) async-start(bf16[2,8,64,3,4,128]{5,4,3,1,0,2:T(4,128)(2,1)} %copy.104), calls=%async_computation.1 | async-start | bytes 6291456 | tf_op jit(solution)/shard_map/all_to_all | solution.py:85
  171.3 0.2 fusion.62
  171.7 143.0 %all-to-all-done.1 = bf16[2,8,64,3,4,128]{5,4,3,1,0,2:T(4,128)(2,1)} async-done(((bf16[2,8,64,3,4,128]{5,4,3,1,0,2:T(4,128)(2,1)}), bf16[2,8,64,3,4,128]{5,4,3,1,0,2:T(4,128)(2,1)}, u32[]{:S(2)}, u32[]{:S(2)}) %all-to-all-start.1) | async-done | bytes 3145760 | tf_op jit(solution)/shard_map/all_to_all | solution.py:85
  314.7 3.0 fusion.59
  317.7 0.3 copy.150
  317.9 0.3 fusion.61
  318.2 0.4 convolution_multiply_fusion
  318.6 0.9 fusion.63
  319.5 0.4 convolution_convert_fusion
  319.9 0.7 fusion.15
  320.6 0.4 multiply_convert_fusion
  321.0 0.4 fusion.13
  321.4 0.5 fusion.12
  321.8 0.3 copy.145
  322.1 0.3 fusion.60
  322.4 0.4 convolution_multiply_fusion.1
  322.8 0.9 fusion.64
  323.7 0.4 convolution_convert_fusion.1
  324.1 0.7 fusion.14
  324.8 0.4 multiply_convert_fusion.1
  325.2 0.4 fusion.11
  325.6 0.5 fusion.10
  326.0 0.3 copy.127
  326.3 0.3 copy.126
  326.6 0.3 copy.125
  326.8 0.3 copy.115
  327.1 0.3 copy.114
  327.4 0.3 copy.113
  327.6 0.3 maximum_maximum_fusion
  328.0 1.8 copy.128
  329.8 7.0 %all-to-all-start.2 = ((bf16[2,8,64,3,3,128]{5,1,3,4,0,2:T(8,128)(2,1)}), bf16[2,8,64,3,3,128]{5,1,3,4,0,2:T(8,128)(2,1)S(1)}, u32[]{:S(2)}, u32[]{:S(2)}) async-start(bf16[2,8,64,3,3,128]{5,1,3,4,0,2:T(8,128)(2,1)} %copy.128), calls=%async_computation.2 | async-start | bytes 4718592 | tf_op jit(solution)/shard_map/all_to_all | solution.py:104
  336.8 1.0 copy.143
  337.8 0.1 copy.141
  338.0 1.5 fusion.31
  339.4 1.3 fusion.27
  340.8 1.3 fusion.26
  342.2 1.3 fusion.22
  343.6 0.6 fusion.29
  344.2 0.6 fusion.24
  344.8 0.6 pad_maximum_fusion.1
  345.4 100.1 %all-to-all-done.2 = bf16[2,8,64,3,3,128]{5,1,3,4,0,2:T(8,128)(2,1)S(1)} async-done(((bf16[2,8,64,3,3,128]{5,1,3,4,0,2:T(8,128)(2,1)}), bf16[2,8,64,3,3,128]{5,1,3,4,0,2:T(8,128)(2,1)S(1)}, u32[]{:S(2)}, u32[]{:S(2)}) %all-to-all-start.2) | async-done | bytes 2359328 | tf_op jit(solution)/shard_map/all_to_all | solution.py:104
  445.5 1.8 copy.129
  447.3 4.3 copy.130
  451.6 6.4 %gather_fusion = bf16[1024,3,128]{2,1,0:T(4,128)(2,1)S(1)} fusion(bf16[2,1536,3,128]{3,2,1,0:T(4,128)(2,1)} %copy.130, s32[1024]{0:T(1024)S(1)} %bitcast.123), kind=kCustom, calls=%fused_computation | custom fusion | bytes 1581056 | tf_op jit(solution)/shard_map/gather | solution.py:105
  458.0 0.1 copy.131
  458.2 1.0 copy.132
  459.1 1.0 copy.133
  460.1 1.0 copy.134
  (48 shorter events, 0.6 us)
Async XLA Ops:
  7.2 41.7 %copy-start = (bf16[2,128,2048]{2,1,0:T(8,128)(2,1)S(1)}, bf16[2,128,2048]{2,1,0:T(8,128)(2,1)}, u32[]{:S(2)}) copy-start(bf16[2,128,2048]{2,1,0:T(8,128)(2,1)} %param.12) | copy-start | bytes 3145732
  7.2 29.1 %copy-start.10 = (bf16[512,2,128]{2,1,0:T(2,128)(2,1)S(1)}, bf16[512,2,128]{2,1,0:T(2,128)(2,1)}, u32[]{:S(2)}) copy-start(bf16[512,2,128]{2,1,0:T(2,128)(2,1)} %param.8) | copy-start | bytes 786436
  7.2 29.2 %copy-start.11 = (bf16[512,2,128]{2,1,0:T(2,128)(2,1)S(1)}, bf16[512,2,128]{2,1,0:T(2,128)(2,1)}, u32[]{:S(2)}) copy-start(bf16[512,2,128]{2,1,0:T(2,128)(2,1)} %param.10) | copy-start | bytes 786436
  7.2 29.2 %copy-start.12 = (bf16[512,2,128]{2,1,0:T(2,128)(2,1)S(1)}, bf16[512,2,128]{2,1,0:T(2,128)(2,1)}, u32[]{:S(2)}) copy-start(bf16[512,2,128]{2,1,0:T(2,128)(2,1)} %param.9) | copy-start | bytes 786436
  7.2 41.7 %all-gather.2.cloned.1.call-start = ((), (), s32[]{:S(2)}) async-start(), calls=%async_computation.3 | async-start | bytes 2359296 | tf_op jit(solution)/shard_map/all_gather | solution.py:59
  17.6 137.5 %all-to-all-start = ((s32[2,8,64,3]{1,0,3,2:T(2,128)}), s32[2,8,64,3]{1,0,3,2:T(2,128)S(1)}, u32[]{:S(2)}, u32[]{:S(2)}) async-start(s32[2,8,64,3]{1,0,3,2:T(2,128)} %copy.98), calls=%async_computation | async-start | bytes 393216 | tf_op jit(solution)/shard_map/all_to_all | solution.py:86
  155.1 159.6 %all-to-all-start.1 = ((bf16[2,8,64,3,4,128]{5,4,3,1,0,2:T(4,128)(2,1)}), bf16[2,8,64,3,4,128]{5,4,3,1,0,2:T(4,128)(2,1)}, u32[]{:S(2)}, u32[]{:S(2)}) async-start(bf16[2,8,64,3,4,128]{5,4,3,1,0,2:T(4,128)(2,1)} %copy.104), calls=%async_computation.1 | async-start | bytes 6291456 | tf_op jit(solution)/shard_map/all_to_all | solution.py:85
  171.5 146.2 %copy-start.9 = (f32[1,8,64,3]{1,0,3,2:T(1,128)}, f32[1,8,64,3]{1,0,3,2:T(1,128)S(1)}, u32[]{:S(2)}) copy-start(f32[1,8,64,3]{1,0,3,2:T(1,128)S(1)} %get-tuple-element.32) | copy-start | bytes 18436
  318.2 2.8 copy-start.5
  318.2 3.1 copy-start.1
  322.4 2.8 copy-start.7
  322.4 3.1 copy-start.3
  329.8 115.7 %all-to-all-start.2 = ((bf16[2,8,64,3,3,128]{5,1,3,4,0,2:T(8,128)(2,1)}), bf16[2,8,64,3,3,128]{5,1,3,4,0,2:T(8,128)(2,1)S(1)}, u32[]{:S(2)}, u32[]{:S(2)}) async-start(bf16[2,8,64,3,3,128]{5,1,3,4,0,2:T(8,128)(2,1)} %copy.128), calls=%async_computation.2 | async-start | bytes 4718592 | tf_op jit(solution)/shard_map/all_to_all | solution.py:104
  337.9 5.6 %copy-start.2 = (bf16[8,192,1,128]{3,0,2,1:T(8,128)(2,1)S(1)}, bf16[8,192,1,128]{3,0,2,1:T(8,128)(2,1)}, u32[]{:S(2)}) copy-start(bf16[8,192,1,128]{3,0,2,1:T(8,128)(2,1)} %copy-done.1) | copy-start | bytes 1179652
  337.9 5.6 %copy-start.6 = (bf16[8,192,1,128]{3,0,2,1:T(8,128)(2,1)S(1)}, bf16[8,192,1,128]{3,0,2,1:T(8,128)(2,1)}, u32[]{:S(2)}) copy-start(bf16[8,192,1,128]{3,0,2,1:T(8,128)(2,1)} %copy-done.5) | copy-start | bytes 1179652
  338.0 6.2 %copy-start.4 = (bf16[8,192,1,128]{3,0,2,1:T(8,128)(2,1)S(1)}, bf16[8,192,1,128]{3,0,2,1:T(8,128)(2,1)}, u32[]{:S(2)}) copy-start(bf16[8,192,1,128]{3,0,2,1:T(8,128)(2,1)} %copy-done.3) | copy-start | bytes 1179652
  338.0 6.2 %copy-start.8 = (bf16[8,192,1,128]{3,0,2,1:T(8,128)(2,1)S(1)}, bf16[8,192,1,128]{3,0,2,1:T(8,128)(2,1)}, u32[]{:S(2)}) copy-start(bf16[8,192,1,128]{3,0,2,1:T(8,128)(2,1)} %copy-done.7) | copy-start | bytes 1179652
Sparse Core Ops, SparseCore 0:
  10.2 38.6 all-gather.1
where the time goes:
time: 471 us; the launch traced here: 468 us
  waiting for transfers between devices  256 us (54%)
  local copies, waits for them, and re-layouts  135 us (29%)
  starting transfers between devices  41.9 us (9%)
  between operations  14.6 us (3%)
  other arithmetic  11.8 us (3%)
  matrix products  8.83 us (2%)
    all_to_all x1, waiting for transfers between devices, on_device(): lax.all_to_all(outgoing[0], 'seq', split_axis=2, concat_axis=2, tiled=True)  143 us
    unnamed x37, local copies, waits for them, and re-layouts  106 us
    all_to_all x1, waiting for transfers between devices, on_device(): lax.all_to_all(outbound, 'seq', split_axis=2, concat_axis=2, tiled=True)  100 us
    all_to_all x1, starting transfers between devices, on_device(): lax.all_to_all(outgoing[1], 'seq', split_axis=2, concat_axis=2, tiled=True)  18.7 us
    all_to_all x1, starting transfers between devices, on_device(): lax.all_to_all(outgoing[0], 'seq', split_axis=2, concat_axis=2, tiled=True)  16.1 us
    all_gather x1, waiting for transfers between devices, on_device(): lax.all_gather(layer_grad, 'head', axis=1, tiled=True)  12.4 us
  transfers between devices with their start and end apart: 4, of which 3 were waited for; matrix products, arithmetic and copies ran while one was open for 27% of the time, Pallas kernels for 0%

commit v1 on v0

v1 whole, which is shorter than its diff:
```python
import functools

import jax
import jax.numpy as jnp
from jax import lax
from jax.experimental import pallas as pl
from jax.experimental.pallas import tpu as pltpu
from jax.sharding import PartitionSpec as P

MESH = pl.DeviceIdType.MESH
CAP = 16
Z = 16
F32 = jnp.float32
BF16 = jnp.bfloat16
UNUSED = 1 << 20


def iota(shape, dim):
    return lax.broadcasted_iota(jnp.int32, shape, dim)


def one_hot(mask):
    return jnp.where(mask, 1.0, 0.0).astype(BF16)


def matmul(a, b):
    return jnp.dot(a, b, preferred_element_type=F32)


def matmul_nt(a, b):
    return lax.dot_general(a, b, (((1,), (1,)), ((), ())), preferred_element_type=F32)


def matmul_tn(a, b):
    return lax.dot_general(a, b, (((0,), (0,)), ((), ())), preferred_element_type=F32)


def kernel(
    n_seq,
    n_head,
    queries,
    keys,
    values,
    layer_grad,
    out_proj,
    cluster,
    slot,
    tile_of,
    query_grad,
    key_grad,
    value_grad,
    centroid,
    gathered,
    grads_out,
    pack,
    unpack,
    qkv_send,
    qkv_recv,
    og_send,
    og_recv,
    meta_send,
    meta_recv,
    ret_send,
    ret_recv,
    key_sum,
    value_sum,
    gather_send_sem,
    gather_recv_sem,
    qkv_send_sem,
    qkv_recv_sem,
    og_send_sem,
    og_recv_sem,
    meta_send_sem,
    meta_recv_sem,
    ret_send_sem,
    ret_recv_sem,
):
    me = lax.axis_index("seq")
    my_head = lax.axis_index("head")
    me_y, me_z = me // Z, me % Z
    n_y = n_seq // Z
    heads, tokens = cluster.shape
    clusters = tile_of.shape[1]
    size = queries.shape[1] // heads
    rows = n_seq * CAP
    columns = layer_grad.shape[1]

    def ahead(k):
        return {"seq": lax.rem(me_y + k // Z, n_y) * Z + lax.rem(me_z + k % Z, Z)}

    def behind(k):
        return {"seq": lax.rem(me_y + n_y - k // Z, n_y) * Z + lax.rem(me_z + Z - k % Z, Z)}

    def peer(j):
        return {"head": lax.rem(my_head + j, n_head)}

    barrier = pltpu.get_barrier_semaphore()

    @pl.loop(1, n_seq)
    def _(k):
        pl.semaphore_signal(barrier, inc=1, device_id=ahead(k), device_id_type=MESH)

    @pl.loop(1, n_head)
    def _(j):
        pl.semaphore_signal(barrier, inc=1, device_id=peer(j), device_id_type=MESH)

    def send(src, dst, send_sem, recv_sem, target):
        pltpu.make_async_remote_copy(
            src_ref=src,
            dst_ref=dst,
            send_sem=send_sem,
            recv_sem=recv_sem,
            device_id=target,
            device_id_type=MESH,
        ).start()

    def send_all(src, dst, send_sem, recv_sem, target):
        @pl.loop(1, n_seq)
        def _(k):
            send(src.at[k], dst.at[k], send_sem, recv_sem, target(k))

    def wait_all(buffer, sem, count):
        part = buffer.at[pl.ds(1, count - 1)]
        pltpu.make_async_copy(part, part, sem).wait()

    earlier = one_hot(iota((tokens, tokens), 0) < iota((tokens, tokens), 1))
    same = one_hot(iota((tokens, tokens), 0) == iota((tokens, tokens), 1))
    meta = jnp.zeros((n_seq, 128), F32)
    for h in range(heads):
        ids = cluster[pl.ds(h, 1), :]
        table = jnp.broadcast_to(tile_of[pl.ds(h, 1), :], (8, clusters))
        table = jnp.where(iota((8, clusters), 0) == 0, table >> 3, table & 7)
        chosen = one_hot(iota((clusters, tokens), 0) == ids)
        found = matmul(table.astype(F32).astype(BF16), chosen).astype(jnp.int32)
        owner, local = found[0:1], found[1:2]
        block = (((owner >> 4) - me_y + n_y) & (n_y - 1)) * Z + (((owner & 15) - me_z + Z) & (Z - 1))
        in_block = iota((n_seq, tokens), 0) == block
        before = matmul(one_hot(in_block), earlier)
        place = jnp.sum(jnp.where(in_block, before, 0.0), axis=0, keepdims=True)
        place_int = place.astype(jnp.int32)
        label = (local * 4 + slot[pl.ds(h, 1), :] + 1).astype(F32)
        labelled = jnp.where(iota((128, tokens), 0) == place_int + CAP * h, label, 0.0).astype(BF16)
        meta += matmul_nt(one_hot(in_block), labelled)
        target = block * CAP + place_int
        pack[h] = one_hot(iota((rows, tokens), 0) == target)
        both = jnp.where(
            iota((8, tokens), 0) == 0, block.astype(F32), jnp.broadcast_to(place, (8, tokens))
        ).astype(BF16)
        both = matmul_nt(same, both).astype(jnp.int32)
        unpack[h] = one_hot(iota((tokens, rows), 1) == both[:, 0:1] * CAP + both[:, 1:2])
    meta_send[...] = meta.reshape(n_seq, 1, 128)

    def pack_part(dst, h, cuts):
        for first in range(0, rows, 256):
            part = pack[h, pl.ds(first, 256), :]
            for i, source in enumerate(cuts):
                moved = matmul(part, source[:, pl.ds(h * size, size)]).astype(BF16)
                dst[h, pl.ds(first // CAP, 256 // CAP), :, pl.ds(i * size, size)] = moved.reshape(
                    256 // CAP, CAP, size
                )

    pack_part(qkv_send, 0, (queries, keys, values))
    pl.semaphore_wait(barrier, n_seq - 1 + n_head - 1)

    @pl.loop(1, n_head)
    def _(j):
        send(layer_grad, gathered.at[j], gather_send_sem, gather_recv_sem, peer(j))

    send_all(meta_send, meta_recv, meta_send_sem, meta_recv_sem, ahead)
    send_all(qkv_send.at[0], qkv_recv.at[0], qkv_send_sem.at[0], qkv_recv_sem.at[0], ahead)
    pack_part(qkv_send, 1, (queries, keys, values))
    meta_recv[0] = meta_send[0]
    for h in range(heads):
        qkv_recv[h, 0] = qkv_send[h, 0]

    wait_all(gathered, gather_recv_sem, n_head)
    total = jnp.zeros((tokens, heads * size), F32)
    for j in range(n_head):
        part = layer_grad[...] if j == 0 else gathered[j]
        source = lax.rem(my_head + n_head - j, n_head)
        weight = out_proj[:, pl.ds(pl.multiple_of(source * columns, columns), columns)]
        total += matmul_nt(part, weight)
    grads_out[...] = total.astype(BF16)
    pack_part(og_send, 0, (grads_out,))
    send_all(og_send.at[0], og_recv.at[0], og_send_sem.at[0], og_recv_sem.at[0], ahead)
    for h in range(1, heads):
        send_all(qkv_send.at[h], qkv_recv.at[h], qkv_send_sem.at[h], qkv_recv_sem.at[h], ahead)
        pack_part(og_send, h, (grads_out,))
        send_all(og_send.at[h], og_recv.at[h], og_send_sem.at[h], og_recv_sem.at[h], ahead)
    for h in range(heads):
        og_recv[h, 0] = og_send[h, 0]

    def codes(index, label):
        k = index >> 4
        source = ((me_y - (k >> 4) + n_y) & (n_y - 1)) * Z + ((me_z - (k & 15) + Z) & (Z - 1))
        used = label > 0
        tile = (label - 1) >> 2
        code = tile * 256 + source * 3 + ((label - 1) & 3)
        return used, tile, code

    factor = size ** (-0.5)
    block_rows = 256
    wait_all(meta_recv, meta_recv_sem, n_seq)
    received = meta_recv[...].reshape(n_seq, 128).astype(BF16)
    for h in range(heads):
        lane_of = one_hot(iota((128, rows), 0) == (iota((128, rows), 1) & 15) + CAP * h)
        spread = matmul(received, lane_of)
        own = iota((n_seq, rows), 0) == iota((n_seq, rows), 1) >> 4
        label_row = jnp.sum(jnp.where(own, spread, 0.0), axis=0, keepdims=True).astype(jnp.int32)
        used_row, tile_row, code_row = codes(iota((1, rows), 1), label_row)
        code_row = jnp.where(used_row, code_row, 2 * UNUSED)
        member = one_hot((iota((8, rows), 0) == tile_row) & used_row)

        wait_all(qkv_recv.at[h], qkv_recv_sem.at[h], n_seq)
        wait_all(og_recv.at[h], og_recv_sem.at[h], n_seq)

        key_sum[...] = jnp.zeros_like(key_sum)
        value_sum[...] = jnp.zeros_like(value_sum)
        every_key = qkv_recv[h, :, :, pl.ds(size, size)].reshape(rows, size)
        every_value = qkv_recv[h, :, :, pl.ds(2 * size, size)].reshape(rows, size)

        @pl.loop(0, rows // block_rows)
        def _(b):
            first = pl.multiple_of(b * (block_rows // CAP), block_rows // CAP)
            chunk = pl.ds(first, block_rows // CAP)
            index = iota((block_rows, n_seq), 0) + b * block_rows
            picked = matmul(one_hot(iota((block_rows, n_seq), 1) == index >> 4), received)
            index = iota((block_rows, 128), 0) + b * block_rows
            lane = iota((block_rows, 128), 1) == (index & 15) + CAP * h
            label = jnp.sum(jnp.where(lane, picked, 0.0), axis=1, keepdims=True).astype(jnp.int32)
            used, tile, code = codes(iota((block_rows, 1), 0) + b * block_rows, label)
            low = jnp.where(used, tile * 256, UNUSED)
            code = jnp.where(used, code, -1)
            query = qkv_recv[h, chunk, :, pl.ds(0, size)].reshape(block_rows, size)
            grad = og_recv[h, chunk, :, :].reshape(block_rows, size)
            scores = matmul_nt(query, every_key) * factor
            allowed = (code_row >= low) & (code_row <= code)
            largest = jnp.max(jnp.where(allowed, scores, -1e30), axis=1, keepdims=True)
            weights = jnp.where(allowed, jnp.exp(scores - largest), 0.0)
            whole = jnp.sum(weights, axis=1, keepdims=True)
            probs = weights / jnp.where(used, whole, 1.0)
            probs_low = probs.astype(BF16)
            dprobs = matmul_nt(grad, every_value)
            stat = jnp.sum(probs_low.astype(F32) * dprobs, axis=1, keepdims=True)
            dscores = (probs * (dprobs - stat)).astype(BF16)
            ret_send[h, chunk, :, pl.ds(0, size)] = (
                (matmul(dscores, every_key) * factor)
                .astype(BF16)
                .reshape(block_rows // CAP, CAP, size)
            )
            key_sum[...] += matmul_tn(dscores, query)
            value_sum[...] += matmul_tn(probs_low, grad)

        ret_send[h, :, :, pl.ds(size, size)] = (
            (key_sum[...] * factor).astype(BF16).reshape(n_seq, CAP, size)
        )
        ret_send[h, :, :, pl.ds(2 * size, size)] = (
            value_sum[...].astype(BF16).reshape(n_seq, CAP, size)
        )
        send_all(ret_send.at[h], ret_recv.at[h], ret_send_sem.at[h], ret_recv_sem.at[h], behind)
        ret_recv[h, 0] = ret_send[h, 0]

        unit = jnp.zeros((rows, size), F32)
        for i in range(2):
            wide = qkv_recv[h, :, :, pl.ds(i * size, size)].reshape(rows, size).astype(F32)
            unit += wide * lax.rsqrt(jnp.sum(wide * wide, axis=1, keepdims=True) + 1e-06)
        high = unit.astype(BF16)
        rest = (unit - high.astype(F32)).astype(BF16)
        centroid[pl.ds(h * 8, 8), :] = matmul(member, high) + matmul(member, rest)

    for h in range(heads):
        wait_all(ret_recv.at[h], ret_recv_sem.at[h], n_seq)
        for i, grad_ref in enumerate((query_grad, key_grad, value_grad)):
            returned = ret_recv[h, :, :, pl.ds(i * size, size)].reshape(rows, size)
            grad_ref[:, pl.ds(h * size, size)] = matmul(unpack[h], returned).astype(BF16)

    wait_all(gathered, gather_send_sem, n_head)
    wait_all(meta_send, meta_send_sem, n_seq)
    for h in range(heads):
        wait_all(qkv_send.at[h], qkv_send_sem.at[h], n_seq)
        wait_all(og_send.at[h], og_send_sem.at[h], n_seq)
        wait_all(ret_send.at[h], ret_send_sem.at[h], n_seq)


def on_device(queries, keys, values, layer_grad, out_proj, cluster, slot, tile_of):
    tokens, heads, size = queries.shape
    n_seq, n_head = lax.axis_size("seq"), lax.axis_size("head")
    rows = n_seq * CAP
    flat = (tokens, heads * size)
    vmem = pl.BlockSpec(memory_space=pltpu.VMEM)
    pair = pltpu.SemaphoreType.DMA((heads,))
    query_grad, key_grad, value_grad, centroid = pl.pallas_call(
        functools.partial(kernel, n_seq, n_head),
        out_shape=[jax.ShapeDtypeStruct(flat, BF16)] * 3
        + [jax.ShapeDtypeStruct((heads * 8, size), F32)],
        in_specs=[vmem] * 8,
        out_specs=[vmem] * 4,
        scratch_shapes=[
            pltpu.VMEM((n_head,) + layer_grad.shape, BF16),
            pltpu.VMEM(flat, BF16),
            pltpu.VMEM((heads, rows, tokens), BF16),
            pltpu.VMEM((heads, tokens, rows), BF16),
            pltpu.VMEM((heads, n_seq, CAP, 3 * size), BF16),
            pltpu.VMEM((heads, n_seq, CAP, 3 * size), BF16),
            pltpu.VMEM((heads, n_seq, CAP, size), BF16),
            pltpu.VMEM((heads, n_seq, CAP, size), BF16),
            pltpu.VMEM((n_seq, 1, 128), F32),
            pltpu.VMEM((n_seq, 1, 128), F32),
            pltpu.VMEM((heads, n_seq, CAP, 3 * size), BF16),
            pltpu.VMEM((heads, n_seq, CAP, 3 * size), BF16),
            pltpu.VMEM((rows, size), F32),
            pltpu.VMEM((rows, size), F32),
            pltpu.SemaphoreType.DMA,
            pltpu.SemaphoreType.DMA,
            pair,
            pair,
            pair,
            pair,
            pltpu.SemaphoreType.DMA,
            pltpu.SemaphoreType.DMA,
            pair,
            pair,
        ],
        compiler_params=pltpu.CompilerParams(
            collective_id=0, has_side_effects=True, vmem_limit_bytes=48 << 20
        ),
        name="routed_attention",
    )(
        queries.reshape(flat),
        keys.reshape(flat),
        values.reshape(flat),
        layer_grad,
        out_proj.reshape(heads * size, -1),
        cluster,
        slot,
        tile_of,
    )
    shape = (tokens, heads, size)
    return (
        query_grad.reshape(shape),
        key_grad.reshape(shape),
        value_grad.reshape(shape),
        centroid.reshape(heads, 8, size),
    )


def solution(mesh):
    in_specs = (
        P("seq", "head", None),
        P("seq", "head", None),
        P("seq", "head", None),
        P("seq", "head"),
        P("head", None, None),
        P("head", "seq"),
        P("head", "seq"),
        P("head", None),
    )
    out_specs = (
        P("seq", "head", None),
        P("seq", "head", None),
        P("seq", "head", None),
        P("head", "seq", None),
    )
    return jax.shard_map(
        on_device, mesh=mesh, in_specs=in_specs, out_specs=out_specs, check_vma=False
    )
```

time: 471 us -> 189 us (0.40)
  waiting for transfers between devices: 256 us -> 0 us
  Pallas kernels: 0 us -> 182 us
  local copies, waits for them, and re-layouts: 135 us -> 5.14 us
  starting transfers between devices: 41.9 us -> 0 us
  between operations: 14.6 us -> 0.73 us
  other arithmetic: 11.8 us -> 0 us
  matrix products: 8.83 us -> 0 us
    all_to_all x3 -> x0, waiting for transfers between devices: 243 us -> none  [the longest x1 143 us: on_device(): lax.all_to_all(outgoing[0], 'seq', split_axis=2, concat_axis=2, tiled=True)]
    pallas_call x0 -> x1, Pallas kernels: none -> 182 us  [on_device(): pl.pallas_call(functools.partial(kernel, n_seq, n_head), out_shape=[jax.S...]
    unnamed x37 -> x12, local copies, waits for them, and re-layouts: 106 us -> 1.7 us
    all_to_all x3 -> x0, starting transfers between devices: 41.9 us -> none  [the longest x1 18.7 us: on_device(): lax.all_to_all(outgoing[1], 'seq', split_axis=2, concat_axis=2, tiled=True)]
    all_gather x1 -> x0, waiting for transfers between devices: 12.4 us -> none  [on_device(): lax.all_gather(layer_grad, 'head', axis=1, tiled=True)]
    dot_general x15 -> x0, matrix products: 8.83 us -> none  [the longest x1 2.33 us: on_device(): jnp.einsum('tm,hdm->thd', lax.all_gather(layer_grad, 'head', axis=1, tile...]
    reshape x4, local copies, waits for them, and re-layouts: 11.5 us -> 3.44 us  [the longest x1 1.14 us: on_device(): values.reshape(flat)]
    reduce_sum x5 -> x0, other arithmetic: 6.66 us -> none  [the longest x2 2.81 us: tile_grads(): jnp.sum(key_wide * key_wide, axis=2, keepdims=True) + 1e-06]
  transfers between devices with their start and end apart: 4 -> 0, of which waited for: 3 -> 0; matrix products, arithmetic and copies ran while one was open for 27% -> 0% of each run, Pallas kernels for 0% -> 0%
where the time goes in v1:
time: 189 us; the launch traced here: 188 us
  Pallas kernels  182 us (96%)
  local copies, waits for them, and re-layouts  5.14 us (3%)
    pallas_call x1, Pallas kernels, on_device(): pl.pallas_call(functools.partial(kernel, n_seq, n_head), out_shape=[jax.S...  182 us

profile of v1, /device:TPU:6, one launch (start us, length us, event | category | flops | bytes accessed | tf_op | source)
XLA Modules:
  0.0 187.8 jit_solution(12499528111609087430)
XLA Ops:
  0.6 0.0 copy-start
  0.6 1.1 copy.18
  1.7 0.0 copy-start.1
  1.7 0.0 copy-start.2
  1.7 0.0 copy-start.3
  1.8 0.0 copy-start.4
  1.8 1.1 copy_bitcast_fusion
  2.9 0.0 copy-done
  2.9 0.0 copy-done.1
  2.9 0.0 copy-done.2
  2.9 0.0 copy-done.3
  2.9 0.0 copy-done.4
  3.0 182.0 %routed_attention.1 = (bf16[512,256]{1,0:T(8,128)(2,1)S(1)}, bf16[512,256]{1,0:T(8,128)(2,1)S(1)}, bf16[512,256]{1,0:T(8,128)(2,1)S(1)}, f32[16,128]{1,0:T(8,128)S(1)}) custom-call(bf16[512,256]{1,0:T(8,128)(2,1)S(1)} %bitcast.13, bf16[512,256]{1,0:T(8,128)(2,1)S(1)} %get-tuple-element.13.keys, bf16[512,256]{1,0:T(8,128)(2,1)S(1)} %get-tuple-element.12.values, ...), custom_call_target="tpu_custom_call" | custom-call | tf_op jit(solution)/shard_map/routed_attention/pallas_call | solution.py:292
  184.9 0.8 reshape.36
  185.7 0.8 reshape.37
  186.5 0.8 reshape.38
  187.2 0.6 copy.20
Async XLA Ops:
  0.6 2.3 %copy-start = (bf16[2,128,2048]{2,1,0:T(8,128)(2,1)S(1)}, bf16[2,128,2048]{2,1,0:T(8,128)(2,1)}, u32[]{:S(2)}) copy-start(bf16[2,128,2048]{2,1,0:T(8,128)(2,1)} %param.12) | copy-start | bytes 3145732
  1.7 1.2 copy-start.1
  1.7 1.2 copy-start.2
  1.7 1.2 copy-start.3
  1.8 1.2 copy-start.4

commit v2 on v1

v2 whole, which is shorter than its diff:
```python
import functools

import jax
import jax.numpy as jnp
from jax import lax
from jax.experimental import pallas as pl
from jax.experimental.pallas import tpu as pltpu
from jax.sharding import PartitionSpec as P

MESH = pl.DeviceIdType.MESH
CAP = 16
Z = 16
F32 = jnp.float32
BF16 = jnp.bfloat16
UNUSED = 1 << 20


def iota(shape, dim):
    return lax.broadcasted_iota(jnp.int32, shape, dim)


def one_hot(mask):
    return jnp.where(mask, 1.0, 0.0).astype(BF16)


def matmul(a, b):
    return jnp.dot(a, b, preferred_element_type=F32)


def matmul_nt(a, b):
    return lax.dot_general(a, b, (((1,), (1,)), ((), ())), preferred_element_type=F32)


def matmul_tn(a, b):
    return lax.dot_general(a, b, (((0,), (0,)), ((), ())), preferred_element_type=F32)


def kernel(
    n_seq,
    n_head,
    *refs,
):
    inputs, outputs, held, results, refs = refs[:8], refs[8:12], refs[12:20], refs[20:24], refs[24:]
    query_grad, key_grad, value_grad, centroid = results
    queries, keys, values, layer_grad, out_proj, cluster, slot, tile_of = held
    (
        gathered,
        grads_out,
        pack,
        unpack,
        rows_send,
        rows_recv,
        meta_send,
        meta_recv,
        ret_send,
        ret_recv,
        key_sum,
        value_sum,
        grads_back,
        gather_send_sem,
        gather_recv_sem,
        meta_send_sem,
        meta_recv_sem,
        send_sem,
        recv_sem,
        held_sem,
        result_sem,
    ) = refs
    me = lax.axis_index("seq")
    my_head = lax.axis_index("head")
    me_y, me_z = me // Z, me % Z
    n_y = n_seq // Z
    heads, tokens = cluster.shape
    clusters = tile_of.shape[1]
    size = queries.shape[2]
    rows = n_seq * CAP
    columns = layer_grad.shape[1]
    others = n_seq - 1

    def ahead(k):
        return {"seq": lax.rem(me_y + k // Z, n_y) * Z + lax.rem(me_z + k % Z, Z)}

    def behind(k):
        return {"seq": lax.rem(me_y + n_y - k // Z, n_y) * Z + lax.rem(me_z + Z - k % Z, Z)}

    def peer(j):
        return {"head": lax.rem(my_head + j, n_head)}

    fetches = [
        pltpu.make_async_copy(source, target, held_sem.at[i])
        for i, (source, target) in enumerate(zip(inputs, held, strict=True))
    ]
    for fetch in fetches[::-1]:
        fetch.start()

    barrier = pltpu.get_barrier_semaphore()

    @pl.loop(1, n_seq)
    def _(k):
        pl.semaphore_signal(barrier, inc=1, device_id=ahead(k), device_id_type=MESH)

    @pl.loop(1, n_head)
    def _(j):
        pl.semaphore_signal(barrier, inc=1, device_id=peer(j), device_id_type=MESH)

    def remote(src, dst, sent, received, target):
        return pltpu.make_async_remote_copy(
            src_ref=src,
            dst_ref=dst,
            send_sem=sent,
            recv_sem=received,
            device_id=target,
            device_id_type=MESH,
        )

    def wait_all(buffer, sem, first, last):
        part = buffer.at[pl.ds(first, last - first)]
        pltpu.make_async_copy(part, part, sem).wait()

    def lanes(ref, h, first, count):
        return ref.at[h, :, :, pl.ds(first * size, count * size)]

    phases = [
        (lanes(rows_send, 0, 0, 3), lanes(rows_recv, 0, 0, 3), ahead, 1, n_seq),
        (lanes(rows_send, 0, 3, 1), lanes(rows_recv, 0, 3, 1), ahead, 1, n_seq),
    ]
    phases += [(rows_send.at[h], rows_recv.at[h], ahead, 1, n_seq) for h in range(1, heads)]
    phases += [
        (ret_send.at[h], ret_recv.at[h], behind, max(1, first), first + n_seq // 2)
        for h in range(heads)
        for first in (0, n_seq // 2)
    ]

    def nth(i):
        return i

    def message(p, i):
        src, dst, target, _, _ = phases[p]
        k = nth(i)
        return remote(src.at[k], dst.at[k], send_sem.at[p], recv_sem.at[p], target(k))

    def issue(p):
        @pl.loop(*phases[p][3:])
        def _(i):
            message(p, i).start()

    def arrived(p):
        _, dst, _, first, last = phases[p]
        wait_all(dst, recv_sem.at[p], first, last)

    places = []

    def route(h):
        ids = cluster[pl.ds(h, 1), :]
        table = jnp.broadcast_to(tile_of[pl.ds(h, 1), :], (8, clusters))
        table = jnp.where(iota((8, clusters), 0) == 0, table >> 3, table & 7)
        chosen = one_hot(iota((clusters, tokens), 0) == ids)
        found = matmul(table.astype(F32).astype(BF16), chosen).astype(jnp.int32)
        owner, local = found[0:1], found[1:2]
        block = (((owner >> 4) - me_y + n_y) & (n_y - 1)) * Z + (((owner & 15) - me_z + Z) & (Z - 1))
        in_block = iota((n_seq, tokens), 0) == block
        earlier = one_hot(iota((tokens, tokens), 0) < iota((tokens, tokens), 1))
        before = matmul(one_hot(in_block), earlier)
        place = jnp.sum(jnp.where(in_block, before, 0.0), axis=0, keepdims=True)
        place_int = place.astype(jnp.int32)
        target = block * CAP + place_int
        places.append((block, place, local))
        pack[h] = one_hot(iota((rows, tokens), 0) == target)

    def labels():
        meta = jnp.zeros((n_seq, 128), F32)
        for h, (block, place, local) in enumerate(places):
            in_block = iota((n_seq, tokens), 0) == block
            label = (local * 4 + slot[pl.ds(h, 1), :] + 1).astype(F32)
            at = iota((128, tokens), 0) == place.astype(jnp.int32) + CAP * h
            meta += matmul_nt(one_hot(in_block), jnp.where(at, label, 0.0).astype(BF16))
        meta_send[...] = meta.reshape(n_seq, 1, 128)

        @pl.loop(1, n_seq)
        def _(k):
            remote(
                meta_send.at[k], meta_recv.at[k], meta_send_sem, meta_recv_sem, ahead(k)
            ).start()

        meta_recv[0] = meta_send[0]

    def route_back(h):
        block, place, _ = places[h]
        same = one_hot(iota((tokens, tokens), 0) == iota((tokens, tokens), 1))
        both = jnp.where(
            iota((8, tokens), 0) == 0, block.astype(F32), jnp.broadcast_to(place, (8, tokens))
        ).astype(BF16)
        both = matmul_nt(same, both).astype(jnp.int32)
        unpack[h] = one_hot(iota((tokens, rows), 1) == both[:, 0:1] * CAP + both[:, 1:2])

    def of_head(ref):
        return lambda h: ref[:, h, :]

    token_rows = [of_head(ref) for ref in (queries, keys, values)]

    def grads_of(h):
        return grads_out[:, pl.ds(h * size, size)]

    def pack_part(h, first_lane, cuts):
        cuts = [cut(h) for cut in cuts]
        for first in range(0, rows, 256):
            part = pack[h, pl.ds(first, 256), :]
            for i, source in enumerate(cuts):
                moved = matmul(part, source).astype(BF16)
                blocks = pl.ds(first // CAP, 256 // CAP)
                moved = moved.reshape(256 // CAP, CAP, size)
                rows_send[h, blocks, :, pl.ds((first_lane + i) * size, size)] = moved

    for fetch in fetches[5:]:
        fetch.wait()
    route(0)
    for fetch in fetches[:5]:
        fetch.wait()
    pack_part(0, 0, token_rows)
    pl.semaphore_wait(barrier, others + n_head - 1)

    @pl.loop(1, n_head)
    def _(j):
        remote(layer_grad, gathered.at[j], gather_send_sem, gather_recv_sem, peer(j)).start()

    issue(0)
    for h in range(1, heads):
        route(h)
    labels()
    for h in range(1, heads):
        pack_part(h, 0, token_rows)

    wait_all(gathered, gather_recv_sem, 1, n_head)
    total = jnp.zeros((tokens, heads * size), F32)
    for j in range(n_head):
        part = layer_grad[...] if j == 0 else gathered[j]
        source = lax.rem(my_head + n_head - j, n_head)
        weight = out_proj[:, pl.ds(pl.multiple_of(source * columns, columns), columns)]
        total += matmul_nt(part, weight)
    grads_out[...] = total.astype(BF16)
    pack_part(0, 3, (grads_of,))
    issue(1)
    for h in range(1, heads):
        pack_part(h, 3, (grads_of,))
    issue(2)
    for h in range(heads):
        rows_recv[h, 0] = rows_send[h, 0]

    def codes(index, label):
        k = index >> 4
        source = ((me_y - (k >> 4) + n_y) & (n_y - 1)) * Z + ((me_z - (k & 15) + Z) & (Z - 1))
        used = label > 0
        tile = (label - 1) >> 2
        code = tile * 256 + source * 3 + ((label - 1) & 3)
        return used, tile, code

    factor = size ** (-0.5)
    block_rows = 256
    turns = rows // block_rows

    def tiles(h):
        received = meta_recv[...].reshape(n_seq, 128).astype(BF16)
        lane_of = one_hot(iota((128, rows), 0) == (iota((128, rows), 1) & 15) + CAP * h)
        spread = matmul(received, lane_of)
        own = iota((n_seq, rows), 0) == iota((n_seq, rows), 1) >> 4
        label_row = jnp.sum(jnp.where(own, spread, 0.0), axis=0, keepdims=True).astype(jnp.int32)
        used_row, tile_row, code_row = codes(iota((1, rows), 1), label_row)
        code_row = jnp.where(used_row, code_row, 2 * UNUSED)
        member = one_hot((iota((8, rows), 0) == tile_row) & used_row)
        key_sum[...] = jnp.zeros_like(key_sum)
        value_sum[...] = jnp.zeros_like(value_sum)
        every_key = rows_recv[h, :, :, pl.ds(size, size)].reshape(rows, size)
        every_value = rows_recv[h, :, :, pl.ds(2 * size, size)].reshape(rows, size)

        @pl.loop(0, turns)
        def _(b):
            start = pl.multiple_of(b * (block_rows // CAP), block_rows // CAP)
            chunk = pl.ds(start, block_rows // CAP)
            index = iota((block_rows, n_seq), 0) + b * block_rows
            picked = matmul(one_hot(iota((block_rows, n_seq), 1) == index >> 4), received)
            index = iota((block_rows, 128), 0) + b * block_rows
            lane = iota((block_rows, 128), 1) == (index & 15) + CAP * h
            label = jnp.sum(jnp.where(lane, picked, 0.0), axis=1, keepdims=True).astype(jnp.int32)
            used, tile, code = codes(iota((block_rows, 1), 0) + b * block_rows, label)
            low = jnp.where(used, tile * 256, UNUSED)
            code = jnp.where(used, code, -1)
            query = rows_recv[h, chunk, :, pl.ds(0, size)].reshape(block_rows, size)
            grad = rows_recv[h, chunk, :, pl.ds(3 * size, size)].reshape(block_rows, size)
            scores = matmul_nt(query, every_key) * factor
            allowed = (code_row >= low) & (code_row <= code)
            largest = jnp.max(jnp.where(allowed, scores, -1e30), axis=1, keepdims=True)
            weights = jnp.where(allowed, jnp.exp(scores - largest), 0.0)
            whole = jnp.sum(weights, axis=1, keepdims=True)
            probs = weights / jnp.where(used, whole, 1.0)
            probs_low = probs.astype(BF16)
            dprobs = matmul_nt(grad, every_value)
            stat = jnp.sum(probs_low.astype(F32) * dprobs, axis=1, keepdims=True)
            dscores = (probs * (dprobs - stat)).astype(BF16)
            ret_send[h, chunk, :, pl.ds(0, size)] = (
                (matmul(dscores, every_key) * factor)
                .astype(BF16)
                .reshape(block_rows // CAP, CAP, size)
            )
            key_sum[...] += matmul_tn(dscores, query)
            value_sum[...] += matmul_tn(probs_low, grad)

        ret_send[h, :, :, pl.ds(size, size)] = (
            (key_sum[...] * factor).astype(BF16).reshape(n_seq, CAP, size)
        )
        ret_send[h, :, :, pl.ds(2 * size, size)] = (
            value_sum[...].astype(BF16).reshape(n_seq, CAP, size)
        )
        ret_recv[h, 0] = ret_send[h, 0]
        return member

    def centroids(h, member):
        unit = jnp.zeros((rows, size), F32)
        for i in range(2):
            wide = rows_recv[h, :, :, pl.ds(i * size, size)].reshape(rows, size).astype(F32)
            unit += wide * lax.rsqrt(jnp.sum(wide * wide, axis=1, keepdims=True) + 1e-06)
        high = unit.astype(BF16)
        rest = (unit - high.astype(F32)).astype(BF16)
        centroid[h] = matmul(member, high) + matmul(member, rest)

    def finish(h, p):
        part = n_seq // 2
        for first in (0, part):
            arrived(p + first // part)
            blocks, columns = pl.ds(first, part), pl.ds(first * CAP, part * CAP)
            returned = ret_recv[h, blocks].reshape(part * CAP, 3 * size)
            moved = matmul(unpack[h, :, columns], returned)
            if first == 0:
                grads_back[...] = moved
            else:
                moved += grads_back[...]
        for i, grad_ref in enumerate((query_grad, key_grad, value_grad)):
            grad_ref[:, h, :] = moved[:, i * size : (i + 1) * size].astype(BF16)

    wait_all(meta_recv, meta_recv_sem, 1, n_seq)
    arrived(0)
    arrived(1)
    member = tiles(0)
    issue(3)
    issue(4)
    centroids(0, member)
    route_back(0)
    arrived(2)
    member = tiles(1)
    issue(5)
    issue(6)
    centroids(1, member)
    route_back(1)
    finish(0, 3)
    finish(1, 5)
    stores = [
        pltpu.make_async_copy(source, target, result_sem.at[i])
        for i, (source, target) in enumerate(zip(results, outputs, strict=True))
    ]
    for store in stores:
        store.start()

    wait_all(gathered, gather_send_sem, 1, n_head)
    wait_all(meta_send, meta_send_sem, 1, n_seq)
    for p, (src, _, _, first, last) in enumerate(phases):
        wait_all(src, send_sem.at[p], first, last)
    for store in stores:
        store.wait()


def copy_out(*refs):
    sources, targets, held, sem = refs[:4], refs[4:8], refs[8:12], refs[12]
    steps = []
    for i, (source, between, target) in enumerate(zip(sources, held, targets, strict=True)):
        fetch = pltpu.make_async_copy(source, between, sem.at[0, i])
        fetch.start()
        steps.append((fetch, pltpu.make_async_copy(between, target, sem.at[1, i])))
    for fetch, store in steps:
        fetch.wait()
        store.start()
    for _, store in steps:
        store.wait()


def on_device(queries, keys, values, layer_grad, out_proj, cluster, slot, tile_of):
    tokens, heads, size = queries.shape
    n_seq, n_head = lax.axis_size("seq"), lax.axis_size("head")
    rows = n_seq * CAP
    flat = (tokens, heads * size)
    out_proj = out_proj.reshape(heads * size, -1)
    arguments = (queries, keys, values, layer_grad, out_proj, cluster, slot, tile_of)
    shapes = [jax.ShapeDtypeStruct((tokens, heads, size), BF16)] * 3
    shapes.append(jax.ShapeDtypeStruct((heads, 8, size), F32))
    results = pl.pallas_call(
        functools.partial(kernel, n_seq, n_head),
        out_shape=shapes,
        in_specs=[pl.BlockSpec(memory_space=pl.ANY)] * 8,
        out_specs=[pl.BlockSpec(memory_space=pl.ANY)] * 4,
        scratch_shapes=[pltpu.VMEM(a.shape, a.dtype) for a in (*arguments, *shapes)]
        + [
            pltpu.VMEM((n_head,) + layer_grad.shape, BF16),
            pltpu.VMEM(flat, BF16),
            pltpu.VMEM((heads, rows, tokens), BF16),
            pltpu.VMEM((heads, tokens, rows), BF16),
            pltpu.VMEM((heads, n_seq, CAP, 4 * size), BF16),
            pltpu.VMEM((heads, n_seq, CAP, 4 * size), BF16),
            pltpu.VMEM((n_seq, 1, 128), F32),
            pltpu.VMEM((n_seq, 1, 128), F32),
            pltpu.VMEM((heads, n_seq, CAP, 3 * size), BF16),
            pltpu.VMEM((heads, n_seq, CAP, 3 * size), BF16),
            pltpu.VMEM((rows, size), F32),
            pltpu.VMEM((rows, size), F32),
            pltpu.VMEM((tokens, 3 * size), F32),
            pltpu.SemaphoreType.DMA,
            pltpu.SemaphoreType.DMA,
            pltpu.SemaphoreType.DMA,
            pltpu.SemaphoreType.DMA,
            pltpu.SemaphoreType.DMA((3 * heads + 1,)),
            pltpu.SemaphoreType.DMA((3 * heads + 1,)),
            pltpu.SemaphoreType.DMA((len(arguments),)),
            pltpu.SemaphoreType.DMA((len(shapes),)),
        ],
        compiler_params=pltpu.CompilerParams(
            collective_id=0, has_side_effects=True, vmem_limit_bytes=60 << 20
        ),
        name="routed_attention",
    )(*arguments)
    return pl.pallas_call(
        copy_out,
        out_shape=shapes,
        in_specs=[pl.BlockSpec(memory_space=pl.ANY)] * 4,
        out_specs=[pl.BlockSpec(memory_space=pl.ANY)] * 4,
        scratch_shapes=[pltpu.VMEM(a.shape, a.dtype) for a in shapes]
        + [pltpu.SemaphoreType.DMA((2, 4))],
        compiler_params=pltpu.CompilerParams(vmem_limit_bytes=60 << 20),
        name="copy_out",
    )(*results)

def solution(mesh):
    in_specs = (
        P("seq", "head", None),
        P("seq", "head", None),
        P("seq", "head", None),
        P("seq", "head"),
        P("head", None, None),
        P("head", "seq"),
        P("head", "seq"),
        P("head", None),
    )
    out_specs = (
        P("seq", "head", None),
        P("seq", "head", None),
        P("seq", "head", None),
        P("head", "seq", None),
    )
    return jax.shard_map(
        on_device, mesh=mesh, in_specs=in_specs, out_specs=out_specs, check_vma=False
    )
```

time: 189 us -> 186 us (0.984)
  local copies, waits for them, and re-layouts: 5.14 us -> 0 us
  Pallas kernels: 182 us -> 185 us
    reshape x4 -> x0, local copies, waits for them, and re-layouts: 3.44 us -> none  [the longest x1 1.14 us: on_device(): values.reshape(flat)]
    pallas_call x1 -> x2, Pallas kernels: 182 us -> 185 us  [the longest x1 183 us: on_device(): pl.pallas_call(functools.partial(kernel, n_seq, n_head), out_shape=shapes...]
where the time goes in v2:
time: 186 us
  Pallas kernels  185 us (99%)
    pallas_call x1, Pallas kernels, on_device(): pl.pallas_call(functools.partial(kernel, n_seq, n_head), out_shape=shapes...  183 us

profile of v2, /device:TPU:6, one launch (start us, length us, event | category | flops | bytes accessed | tf_op | source)
XLA Modules:
  0.0 185.5 jit_solution(10613536850884472681)
XLA Ops:
  0.6 182.8 %routed_attention.1 = (bf16[512,2,128]{2,1,0:T(2,128)(2,1)}, bf16[512,2,128]{2,1,0:T(2,128)(2,1)}, bf16[512,2,128]{2,1,0:T(2,128)(2,1)}, f32[2,8,128]{2,1,0:T(8,128)}) custom-call(bf16[512,2,128]{2,1,0:T(2,128)(2,1)} %refs_0_.1, bf16[512,2,128]{2,1,0:T(2,128)(2,1)} %refs_1_.1, bf16[512,2,128]{2,1,0:T(2,128)(2,1)} %refs_2_.1, bf16[512,256]{1,0:T(8,128)(2,1)} %refs_3_.1, ...), custom_call_target="tpu_custom_call" | custom-call | tf_op jit(solution)/shard_map/routed_attention/pallas_call | solution.py:393
  183.5 1.9 %copy_out.1 = (bf16[512,2,128]{2,1,0:T(2,128)(2,1)}, bf16[512,2,128]{2,1,0:T(2,128)(2,1)}, bf16[512,2,128]{2,1,0:T(2,128)(2,1)}, f32[2,8,128]{2,1,0:T(8,128)}) custom-call(bf16[512,2,128]{2,1,0:T(2,128)(2,1)} %get-tuple-element.8.refs_0_, bf16[512,2,128]{2,1,0:T(2,128)(2,1)} %get-tuple-element.9.refs_1_, bf16[512,2,128]{2,1,0:T(2,128)(2,1)} %get-tuple-element.10.refs_2_, ...), custom_call_target="tpu_custom_call" | custom-call | tf_op jit(solution)/shard_map/copy_out/pallas_call | solution.py:427

commit v3 on v2

--- a/solution.py
+++ b/solution.py
@@ -139,8 +139,8 @@
         k = nth(i)
         return remote(src.at[k], dst.at[k], send_sem.at[p], recv_sem.at[p], target(k))
 
-    def issue(p):
-        @pl.loop(*phases[p][3:])
+    def issue(p, first=None, last=None):
+        @pl.loop(first or phases[p][3], last or phases[p][4])
         def _(i):
             message(p, i).start()
 
@@ -164,12 +164,11 @@
         place = jnp.sum(jnp.where(in_block, before, 0.0), axis=0, keepdims=True)
         place_int = place.astype(jnp.int32)
         target = block * CAP + place_int
-        places.append((block, place, local))
-        pack[h] = one_hot(iota((rows, tokens), 0) == target)
+        places.append((block, place, local, target))
 
     def labels():
         meta = jnp.zeros((n_seq, 128), F32)
-        for h, (block, place, local) in enumerate(places):
+        for h, (block, place, local, _) in enumerate(places):
             in_block = iota((n_seq, tokens), 0) == block
             label = (local * 4 + slot[pl.ds(h, 1), :] + 1).astype(F32)
             at = iota((128, tokens), 0) == place.astype(jnp.int32) + CAP * h
@@ -185,7 +184,7 @@
         meta_recv[0] = meta_send[0]
 
     def route_back(h):
-        block, place, _ = places[h]
+        block, place, _, _ = places[h]
         same = one_hot(iota((tokens, tokens), 0) == iota((tokens, tokens), 1))
         both = jnp.where(
             iota((8, tokens), 0) == 0, block.astype(F32), jnp.broadcast_to(place, (8, tokens))
@@ -201,31 +200,48 @@
     def grads_of(h):
         return grads_out[:, pl.ds(h * size, size)]
 
+    step = 256
+
+    def pack_step(h, first, first_lane, cuts):
+        part = pack[h, pl.ds(first, step), :]
+        for i, source in enumerate(cuts):
+            moved = matmul(part, source).astype(BF16).reshape(step // CAP, CAP, size)
+            blocks = pl.ds(first // CAP, step // CAP)
+            rows_send[h, blocks, :, pl.ds((first_lane + i) * size, size)] = moved
+
     def pack_part(h, first_lane, cuts):
         cuts = [cut(h) for cut in cuts]
-        for first in range(0, rows, 256):
-            part = pack[h, pl.ds(first, 256), :]
-            for i, source in enumerate(cuts):
-                moved = matmul(part, source).astype(BF16)
-                blocks = pl.ds(first // CAP, 256 // CAP)
-                moved = moved.reshape(256 // CAP, CAP, size)
-                rows_send[h, blocks, :, pl.ds((first_lane + i) * size, size)] = moved
+        for first in range(0, rows, step):
+            pack_step(h, first, first_lane, cuts)
+
+    def select(h, first):
+        at = iota((step, tokens), 0) + first
+        pack[h, pl.ds(first, step), :] = one_hot(at == places[h][3])
 
     for fetch in fetches[5:]:
         fetch.wait()
     route(0)
     for fetch in fetches[:5]:
         fetch.wait()
-    pack_part(0, 0, token_rows)
-    pl.semaphore_wait(barrier, others + n_head - 1)
-
-    @pl.loop(1, n_head)
-    def _(j):
-        remote(layer_grad, gathered.at[j], gather_send_sem, gather_recv_sem, peer(j)).start()
-
-    issue(0)
+    cuts = [cut(0) for cut in token_rows]
+    for first in range(0, rows, step):
+        select(0, first)
+        pack_step(0, first, 0, cuts)
+        if first == 0:
+            pl.semaphore_wait(barrier, others + n_head - 1)
+        issue(0, max(1, first // CAP), (first + step) // CAP)
+        if first == 0:
+
+            @pl.loop(1, n_head)
+            def _(j):
+                remote(
+                    layer_grad, gathered.at[j], gather_send_sem, gather_recv_sem, peer(j)
+                ).start()
+
     for h in range(1, heads):
         route(h)
+        for first in range(0, rows, step):
+            select(h, first)
     labels()
     for h in range(1, heads):
         pack_part(h, 0, token_rows)
@@ -322,6 +338,11 @@
         rest = (unit - high.astype(F32)).astype(BF16)
         centroid[h] = matmul(member, high) + matmul(member, rest)
 
+    stores = [
+        pltpu.make_async_copy(source, target, result_sem.at[i])
+        for i, (source, target) in enumerate(zip(results, outputs, strict=True))
+    ]
+
     def finish(h, p):
         part = n_seq // 2
         for first in (0, part):
@@ -335,6 +356,8 @@
                 moved += grads_back[...]
         for i, grad_ref in enumerate((query_grad, key_grad, value_grad)):
             grad_ref[:, h, :] = moved[:, i * size : (i + 1) * size].astype(BF16)
+            if h == heads - 1:
+                stores[i].start()
 
     wait_all(meta_recv, meta_recv_sem, 1, n_seq)
     arrived(0)
@@ -350,14 +373,9 @@
     issue(6)
     centroids(1, member)
     route_back(1)
+    stores[3].start()
     finish(0, 3)
     finish(1, 5)
-    stores = [
-        pltpu.make_async_copy(source, target, result_sem.at[i])
-        for i, (source, target) in enumerate(zip(results, outputs, strict=True))
-    ]
-    for store in stores:
-        store.start()
 
     wait_all(gathered, gather_send_sem, 1, n_head)
     wait_all(meta_send, meta_send_sem, 1, n_seq)

time: 186 us -> 185 us (level)
  no operation moved by 1% of the time
where the time goes in v3:
time: 185 us
  Pallas kernels  184 us (99%)
    pallas_call x1, Pallas kernels, on_device(): pl.pallas_call(functools.partial(kernel, n_seq, n_head), out_shape=shapes...  183 us

profile of v3, /device:TPU:6, one launch (start us, length us, event | category | flops | bytes accessed | tf_op | source)
XLA Modules:
  0.0 185.2 jit_solution(6612797984314489813)
XLA Ops:
  0.6 182.5 %routed_attention.1 = (bf16[512,2,128]{2,1,0:T(2,128)(2,1)}, bf16[512,2,128]{2,1,0:T(2,128)(2,1)}, bf16[512,2,128]{2,1,0:T(2,128)(2,1)}, f32[2,8,128]{2,1,0:T(8,128)}) custom-call(bf16[512,2,128]{2,1,0:T(2,128)(2,1)} %refs_0_.1, bf16[512,2,128]{2,1,0:T(2,128)(2,1)} %refs_1_.1, bf16[512,2,128]{2,1,0:T(2,128)(2,1)} %refs_2_.1, bf16[512,256]{1,0:T(8,128)(2,1)} %refs_3_.1, ...), custom_call_target="tpu_custom_call" | custom-call | tf_op jit(solution)/shard_map/routed_attention/pallas_call | solution.py:411
  183.2 1.9 %copy_out.1 = (bf16[512,2,128]{2,1,0:T(2,128)(2,1)}, bf16[512,2,128]{2,1,0:T(2,128)(2,1)}, bf16[512,2,128]{2,1,0:T(2,128)(2,1)}, f32[2,8,128]{2,1,0:T(8,128)}) custom-call(bf16[512,2,128]{2,1,0:T(2,128)(2,1)} %get-tuple-element.8.refs_0_, bf16[512,2,128]{2,1,0:T(2,128)(2,1)} %get-tuple-element.9.refs_1_, bf16[512,2,128]{2,1,0:T(2,128)(2,1)} %get-tuple-element.10.refs_2_, ...), custom_call_target="tpu_custom_call" | custom-call | tf_op jit(solution)/shard_map/copy_out/pallas_call | solution.py:445
